TPU v7x, 32 devices: a whole 2x2x4 slice. The times are simulated.
32 devices in a mesh: row: 4 (over x, core), col: 8 (over z, y).
Axes of the slice: x: 2, y: 2, z: 4, core: 2. Of those that a mesh axis runs over, the one named last changes fastest.
Arguments:
- coefs: bfloat16 [1024, 4096], P('col', 'row'), may hold values from -6 to 6
- direction: bfloat16 [1024, 4096], P('col', 'row'), may hold values from -6 to 6
- tiles: bfloat16 [4, 192, 4096], P('row', 'col'), may hold values from -0.3125 to 0.3125
- block_rows: int32 [4, 192], P('row', 'col'), may hold values from 0 to 15
- block_cols: int32 [4, 192], P('row', 'col'), may hold values from 0 to 63
- counts: int32 [4, 8], P('row', 'col'), may hold values from 3 to 24, as said below
Outputs:
- h_coefs: bfloat16 [1024, 4096], P('col', 'row')
- h_direction: bfloat16 [1024, 4096], P('col', 'row')
Inputs may be any that keep to these rules, and one draw needn't show every extreme that they name: `counts`: each value lies between 3 and 24; some device's list is full in every draw. `block_cols`: tiles of one device may repeat a place.
All inputs are finite; a program needn't handle non-finite values.
Results may differ from a plain program's by a relative error of at most 0.008.
Values may be sent and summed in bfloat16 or wider, within the bound.
A program may use at most 128 MiB of HBM per device.

v0:
```python
import functools

import jax
import jax.numpy as jnp
from jax import lax
from jax.experimental import pallas as pl
from jax.experimental.pallas import tpu as pltpu
from jax.sharding import PartitionSpec as P

BLOCK = 64
X_CHUNKS = 4
HALVES = 2
MESH = pl.DeviceIdType.MESH


def kernel(n_row, n_col, coef, direc, tiles, rows, cols, counts, out_c, out_d,
           xall, tall, mall, smeta, sums, acc, flat, rows2,
           sib_s, sib_r, cross_s, cross_r, fwd_s, fwd_r, ring_s, ring_r, meta_s, meta_r, loc):
    orbs, basis = coef.shape
    width = 2 * orbs
    slots = rows.shape[1]
    blocks = basis // BLOCK
    pairs = slots // 2
    cut_pairs = pairs // HALVES
    chips = n_row // 2
    steps = n_col // 2
    part = basis // X_CHUNKS
    per = part // BLOCK

    me_r, me_c = lax.axis_index("row"), lax.axis_index("col")
    chip, core = me_r // 2, me_r % 2
    sibling = chip * 2 + 1 - core
    turn = me_c % 2
    pos = me_c // 2 + turn * (n_col - 1 - 2 * (me_c // 2))

    def at_pos(p):
        side = p // steps
        return 2 * (p + side * (n_col - 1 - 2 * p)) + side

    nxt, prv = at_pos((pos + 1) % n_col), at_pos((pos + n_col - 1) % n_col)

    barrier = pltpu.get_barrier_semaphore()
    for c in (nxt, prv):
        pl.semaphore_signal(barrier, inc=1, device_id=(me_r, c), device_id_type=MESH)
    pl.semaphore_signal(barrier, inc=1, device_id=(sibling, me_c), device_id_type=MESH)
    for k in range(1, chips):
        pl.semaphore_signal(barrier, inc=1, device_id=(((chip + k) % chips) * 2 + core, me_c), device_id_type=MESH)

    for m in range(BLOCK // 2):
        flat[:, m, :] = tiles[0, :, m * 2 * BLOCK:(m + 1) * 2 * BLOCK].astype(jnp.float32)

    lane1 = lax.broadcasted_iota(jnp.int32, (1, 128), 1)
    pad = lax.broadcasted_iota(jnp.int32, (8, 128), 0)
    row_key = jnp.where(lane1[:, :slots] < counts[0, 0], rows[...], blocks)
    mall[0] = jnp.zeros((8, 128), jnp.int32)
    mall[0, 0:1, 0:slots] = row_key * slots + lane1[:, :slots]
    mall[0, 1:2, 0:slots] = cols[...]
    mall[0, 2:3, 0:slots] = row_key
    wide = mall[0]
    tall_form = wide.T
    key_col, col_col, row_col = (tall_form[:slots, i:i + 1] for i in range(3))
    rank = jnp.sum((key_col < wide[0:1]).astype(jnp.int32), axis=0, keepdims=True)
    rank_col = jnp.where(pad == 0, rank, 0).T[:slots, 0:1]
    hit = rank_col == lane1

    def pull(values):
        return jnp.sum(jnp.where(hit, values, 0), axis=0, keepdims=True)

    source = pull(lax.broadcasted_iota(jnp.int32, (slots, 128), 0))
    upto = jnp.sum((row_col <= lane1).astype(jnp.int32), axis=0, keepdims=True)
    have = jnp.sum((row_col == lane1).astype(jnp.int32), axis=0, keepdims=True)
    for i, values in enumerate((pull(row_col), pull(col_col), jnp.maximum(upto - 1, 0), have, source)):
        mall[0, i:i + 1] = values
    to_smem = [pltpu.make_async_copy(mall.at[i], smeta.at[i], loc.at[i]) for i in range(n_col)]
    to_smem[0].start()
    base = me_r * blocks
    for c in range(X_CHUNKS):
        for a, src in enumerate((coef, direc)):
            piece = src[:, c * part:(c + 1) * part].astype(jnp.float32).T.astype(jnp.bfloat16)
            xall[pl.ds(base + c * per, per), :, a * orbs:(a + 1) * orbs] = piece.reshape(per, BLOCK, orbs)
    lane = lax.broadcasted_iota(jnp.int32, (16, 2 * BLOCK), 1)

    first = lax.broadcasted_iota(jnp.int32, (BLOCK // 2, 2 * BLOCK), 1) < BLOCK
    to_smem[0].wait()
    for k in range(pairs):
        one, two = flat[smeta[0, 4, 2 * k]], flat[smeta[0, 4, 2 * k + 1]]
        rows2[pl.ds(0, BLOCK // 2, stride=2), :] = jnp.where(first, one, pltpu.roll(two, BLOCK, 1))
        rows2[pl.ds(1, BLOCK // 2, stride=2), :] = jnp.where(first, pltpu.roll(one, BLOCK, 1), two)
        tall[0, k] = rows2[...].astype(jnp.bfloat16)
    pl.semaphore_wait(barrier, 2 + 1 + chips - 1)

    def x_ref(owner, c):
        return xall.at[pl.ds(owner * blocks + c * per, per)]

    def x_copy(owner, c, to, send, recv):
        return pltpu.make_async_remote_copy(
            src_ref=x_ref(owner, c), dst_ref=x_ref(owner, c), send_sem=send, recv_sem=recv,
            device_id=(to, me_c), device_id_type=MESH)

    def cross_to(k, c):
        return x_copy(me_r, c, ((chip + k) % chips) * 2 + core, cross_s.at[k - 1, c], cross_r.at[k - 1, c])

    def cross_from(k, c):
        owner = ((chip + chips - k) % chips) * 2 + core
        return x_copy(owner, c, owner, cross_s.at[k - 1, c], cross_r.at[k - 1, c])

    def sib_to(c):
        return x_copy(me_r, c, sibling, sib_s.at[c], sib_r.at[c])

    def sib_from(c):
        return x_copy(sibling, c, sibling, sib_s.at[c], sib_r.at[c])

    def fwd_to(k, c):
        owner = ((chip + chips - k) % chips) * 2 + core
        return x_copy(owner, c, sibling, fwd_s.at[k - 1, c], fwd_r.at[k - 1, c])

    def fwd_from(k, c):
        owner = ((chip + chips - k) % chips) * 2 + 1 - core
        return x_copy(owner, c, sibling, fwd_s.at[k - 1, c], fwd_r.at[k - 1, c])

    def ring_slots(d, t):
        return (t - 1, t) if d == 0 else ((n_col - t + 1) % n_col, n_col - t)

    def ring(d, t, h):
        a, b = ring_slots(d, t)
        cut = pl.ds(h * cut_pairs, cut_pairs)
        return pltpu.make_async_remote_copy(
            src_ref=tall.at[a, cut], dst_ref=tall.at[b, cut],
            send_sem=ring_s.at[d, t - 1, h], recv_sem=ring_r.at[d, t - 1, h],
            device_id=(me_r, nxt if d == 0 else prv), device_id_type=MESH)

    def meta(d, t):
        a, b = ring_slots(d, t)
        return pltpu.make_async_remote_copy(
            src_ref=mall.at[a], dst_ref=mall.at[b],
            send_sem=meta_s.at[d, t - 1], recv_sem=meta_r.at[d, t - 1],
            device_id=(me_r, nxt if d == 0 else prv), device_id_type=MESH)

    def ring_parts(t):
        if t < steps:
            return [(d, h) for h in range(HALVES) for d in (0, 1)], (0, 1)
        return [(0, 0), (1, 1)], (0,)

    def slot_of(q):
        return (q % 2) * ((q + 1) // 2) + (1 - q % 2) * ((n_col - q // 2) % n_col)

    def compute(q):
        slot = slot_of(q)
        carry = None
        for g in range(slots // 4):
            r = [smeta[slot, 0, 4 * g + i] for i in range(4)]
            blank = jnp.zeros((BLOCK, 2 * BLOCK), jnp.bfloat16)
            grid = []
            for a in range(4):
                line = []
                for u in range(2):
                    if a < 2 * u:
                        line.append(blank)
                        continue
                    lead = lane < BLOCK
                    keep = lead if a == 2 * u else jnp.where(lead, r[2 * u], r[2 * u + 1]) == r[a]
                    keep = jnp.where(keep, 1.0, 0.0).astype(jnp.bfloat16)
                    mats = tall[slot, 2 * g + u].reshape(BLOCK // 16, 16, 2 * BLOCK)
                    line.append((mats * keep[None]).reshape(BLOCK, 2 * BLOCK))
                grid.append(jnp.concatenate(line, axis=1))
            picked = jnp.concatenate([xall[smeta[slot, 1, 4 * g + i]] for i in range(4)], axis=0)
            got = jnp.dot(jnp.concatenate(grid, axis=0), picked, preferred_element_type=jnp.float32)
            for a in range(4):
                one = got[a * BLOCK:(a + 1) * BLOCK]
                if carry is not None:
                    one = one + jnp.where(r[a] == before, carry, 0.0)
                sums[4 * g + a] = one
            carry, before = one, r[3]
        for b in range(blocks):
            at = slice(b * BLOCK, (b + 1) * BLOCK)
            acc[at, :] += jnp.where(smeta[slot, 3, b] > 0, sums[smeta[slot, 2, b]], 0.0)

    def send_ring(t):
        pieces, metas = ring_parts(t)
        for d in metas:
            meta(d, t).start()
        for d, h in pieces:
            ring(d, t, h).start()

    def ring_event(t):
        pieces, metas = ring_parts(t)
        more, more_metas = ring_parts(t + 1) if t < steps else ((), ())
        for d in metas:
            meta(d, t).wait_recv()
            if d in more_metas:
                meta(d, t + 1).start()
        for d, h in pieces:
            ring(d, t, h).wait_recv()
            if (d, h) in more:
                ring(d, t + 1, h).start()
        for d in metas:
            to_smem[ring_slots(d, t)[1]].start()

    for c in range(X_CHUNKS):
        for k in range(1, chips):
            cross_to(k, c).start()
        if c == 0:
            send_ring(1)
    for c in range(X_CHUNKS):
        sib_to(c).start()
    acc[...] = jnp.zeros_like(acc)

    events = [(((k - 1) * X_CHUNKS + c + 1) * 2.6, 0, k, c) for k in range(1, chips) for c in range(X_CHUNKS)]
    events += [(t * 3.9, 1, t, 0) for t in range(1, steps)]
    for _, kind, k, c in sorted(events):
        if kind == 0:
            cross_from(k, c).wait_recv()
            fwd_to(k, c).start()
        else:
            ring_event(k)
    for c in range(X_CHUNKS):
        sib_from(c).wait_recv()
    for k in range(1, chips):
        for c in range(X_CHUNKS):
            fwd_from(k, c).wait_recv()

    for t in range(1, steps):
        for d in (0, 1):
            to_smem[ring_slots(d, t)[1]].wait()

    def shard(q, carry):
        compute(q)
        return carry

    lax.fori_loop(0, n_col - 1, shard, 0)
    ring_event(steps)
    to_smem[steps].wait()
    lax.fori_loop(n_col - 1, n_col, shard, 0)

    for a, out in enumerate((out_c, out_d)):
        for m in range(basis // 256):
            out[:, m * 256:(m + 1) * 256] = acc[m * 256:(m + 1) * 256, a * orbs:(a + 1) * orbs].T.astype(jnp.bfloat16)

    for c in range(X_CHUNKS):
        sib_to(c).wait_send()
        for k in range(1, chips):
            cross_to(k, c).wait_send()
            fwd_to(k, c).wait_send()
    for t in range(1, steps + 1):
        pieces, metas = ring_parts(t)
        for d in metas:
            meta(d, t).wait_send()
        for d, h in pieces:
            ring(d, t, h).wait_send()


def hand_over(a, b, out_a, out_b, sems):
    copies = [pltpu.make_async_copy(src, dst, sems.at[i]) for i, (src, dst) in enumerate(((a, out_a), (b, out_b)))]
    for copy in copies:
        copy.start()
    for copy in copies:
        copy.wait()


def local(n_row, n_col, coefs, direction, tiles, block_rows, block_cols, counts):
    slots = tiles.shape[1]
    orbs, basis = coefs.shape
    width = 2 * orbs
    chips, steps = n_row // 2, n_col // 2
    vmem = pl.BlockSpec(memory_space=pltpu.VMEM)
    dma = pltpu.SemaphoreType.DMA
    out = jax.ShapeDtypeStruct((orbs, basis), jnp.bfloat16)
    results = pl.pallas_call(
        functools.partial(kernel, n_row, n_col),
        out_shape=(out, out),
        in_specs=[vmem] * 5 + [pl.BlockSpec(memory_space=pltpu.SMEM)],
        out_specs=(vmem, vmem),
        scratch_shapes=[
            pltpu.VMEM((n_row * basis // BLOCK, BLOCK, width), jnp.bfloat16),
            pltpu.VMEM((n_col, slots // 2, BLOCK, 2 * BLOCK), jnp.bfloat16),
            pltpu.VMEM((n_col, 8, 128), jnp.int32),
            pltpu.SMEM((n_col, 8, 128), jnp.int32),
            pltpu.VMEM((slots, BLOCK, width), jnp.float32),
            pltpu.VMEM((basis, width), jnp.float32),
            pltpu.VMEM((slots, BLOCK // 2, 2 * BLOCK), jnp.float32),
            pltpu.VMEM((BLOCK, 2 * BLOCK), jnp.float32),
            dma((X_CHUNKS,)), dma((X_CHUNKS,)),
            dma((chips - 1, X_CHUNKS)), dma((chips - 1, X_CHUNKS)),
            dma((chips - 1, X_CHUNKS)), dma((chips - 1, X_CHUNKS)),
            dma((2, steps, HALVES)), dma((2, steps, HALVES)),
            dma((2, steps)), dma((2, steps)),
            dma((n_col,)),
        ],
        compiler_params=pltpu.CompilerParams(
            collective_id=0, has_side_effects=True, vmem_limit_bytes=56 * 2**20),
        name="block_sparse_apply",
    )(coefs, direction, tiles, block_rows, block_cols, counts)
    return tuple(pl.pallas_call(
        hand_over,
        out_shape=(out, out),
        in_specs=[pl.BlockSpec(memory_space=pl.ANY)] * 2,
        out_specs=(pl.BlockSpec(memory_space=pl.ANY),) * 2,
        scratch_shapes=[dma((2,))],
        name="hand_over",
    )(*results))


def solution(mesh):
    body = functools.partial(local, mesh.shape["row"], mesh.shape["col"])
    return jax.shard_map(
        body,
        mesh=mesh,
        in_specs=(
            P("col", "row"),
            P("col", "row"),
            P("row", "col", None),
            P("row", "col"),
            P("row", "col"),
            P("row", "col"),
        ),
        out_specs=(P("col", "row"), P("col", "row")),
        check_vma=False,
    )
```

profile of v0, /device:TPU:0, one launch (start us, length us, event | category | flops | bytes accessed | tf_op | source)
XLA Modules:
  0.0 46.7 jit_solution(1112734344470085370)
XLA Ops:
  1.3 28.4 %block_sparse_apply.1 = (bf16[128,1024]{1,0:T(8,128)(2,1)}, bf16[128,1024]{1,0:T(8,128)(2,1)}) custom-call(bf16[128,1024]{1,0:T(8,128)(2,1)} %coef.1, bf16[128,1024]{1,0:T(8,128)(2,1)} %direc.1, bf16[1,24,4096]{2,1,0:T(8,128)(2,1)} %tiles.1, s32[1,24]{1,0:T(1,128)} %rows.1, s32[1,24]{1,0:T(1,128)} %cols.1, s32[1,1]{1,0:T(1,128)S(6)} %copy.8.counts), custom_call_target="tpu_custom_call" | custom-call | tf_op jit(solution)/shard_map/block_sparse_apply/pallas_call | solution.py:268
  29.7 17.0 %hand_over.1 = (bf16[128,1024]{1,0:T(8,128)(2,1)}, bf16[128,1024]{1,0:T(8,128)(2,1)}) custom-call(bf16[128,1024]{1,0:T(8,128)(2,1)} %get-tuple-element.4.a, bf16[128,1024]{1,0:T(8,128)(2,1)} %get-tuple-element.5.b), custom_call_target="tpu_custom_call" | custom-call | tf_op jit(solution)/shard_map/hand_over/pallas_call | solution.py:293
where the time goes:
time: 46.8 us; the launch traced here: 46.7 us
  Pallas kernels  45.4 us (97%)
  between operations  1.29 us (3%)
    pallas_call x1, Pallas kernels, local(): pl.pallas_call(functools.partial(kernel, n_row, n_col), out_shape=(out, o...  28.4 us
    pallas_call x1, Pallas kernels, local(): pl.pallas_call(hand_over, out_shape=(out, out), in_specs=[pl.BlockSpec(me...  17 us

commit v1 on v0

--- a/solution.py
+++ b/solution.py
@@ -8,7 +8,7 @@
 from jax.sharding import PartitionSpec as P
 
 BLOCK = 64
-X_CHUNKS = 4
+X_CHUNKS = 2
 HALVES = 2
 MESH = pl.DeviceIdType.MESH
 
@@ -26,6 +26,7 @@
     steps = n_col // 2
     part = basis // X_CHUNKS
     per = part // BLOCK
+    x_parts = [(a, c) for a in (0, 1) for c in range(X_CHUNKS)]
 
     me_r, me_c = lax.axis_index("row"), lax.axis_index("col")
     chip, core = me_r // 2, me_r % 2
@@ -45,9 +46,6 @@
     pl.semaphore_signal(barrier, inc=1, device_id=(sibling, me_c), device_id_type=MESH)
     for k in range(1, chips):
         pl.semaphore_signal(barrier, inc=1, device_id=(((chip + k) % chips) * 2 + core, me_c), device_id_type=MESH)
-
-    for m in range(BLOCK // 2):
-        flat[:, m, :] = tiles[0, :, m * 2 * BLOCK:(m + 1) * 2 * BLOCK].astype(jnp.float32)
 
     lane1 = lax.broadcasted_iota(jnp.int32, (1, 128), 1)
     pad = lax.broadcasted_iota(jnp.int32, (8, 128), 0)
@@ -60,37 +58,33 @@
     tall_form = wide.T
     key_col, col_col, row_col = (tall_form[:slots, i:i + 1] for i in range(3))
     rank = jnp.sum((key_col < wide[0:1]).astype(jnp.int32), axis=0, keepdims=True)
+    moves = jnp.where(rank[:, :slots] == lax.broadcasted_iota(jnp.int32, (slots, slots), 0), 1.0, 0.0)
+    in_order = jnp.dot(moves.astype(jnp.bfloat16), tiles[0], preferred_element_type=jnp.float32)
+    for m in range(BLOCK // 2):
+        flat[:, m, :] = in_order[:, m * 2 * BLOCK:(m + 1) * 2 * BLOCK]
+    first = lax.broadcasted_iota(jnp.int32, (BLOCK // 2, 2 * BLOCK), 1) < BLOCK
+    for k in range(pairs):
+        one, two = flat[2 * k], flat[2 * k + 1]
+        rows2[k, pl.ds(0, BLOCK // 2, stride=2), :] = jnp.where(first, one, pltpu.roll(two, BLOCK, 1))
+        rows2[k, pl.ds(1, BLOCK // 2, stride=2), :] = jnp.where(first, pltpu.roll(one, BLOCK, 1), two)
+        tall[0, k] = rows2[k].astype(jnp.bfloat16)
     rank_col = jnp.where(pad == 0, rank, 0).T[:slots, 0:1]
     hit = rank_col == lane1
 
     def pull(values):
         return jnp.sum(jnp.where(hit, values, 0), axis=0, keepdims=True)
 
-    source = pull(lax.broadcasted_iota(jnp.int32, (slots, 128), 0))
     upto = jnp.sum((row_col <= lane1).astype(jnp.int32), axis=0, keepdims=True)
     have = jnp.sum((row_col == lane1).astype(jnp.int32), axis=0, keepdims=True)
-    for i, values in enumerate((pull(row_col), pull(col_col), jnp.maximum(upto - 1, 0), have, source)):
+    for i, values in enumerate((pull(row_col), pull(col_col), jnp.maximum(upto - 1, 0), have)):
         mall[0, i:i + 1] = values
     to_smem = [pltpu.make_async_copy(mall.at[i], smeta.at[i], loc.at[i]) for i in range(n_col)]
-    to_smem[0].start()
+    lane = lax.broadcasted_iota(jnp.int32, (16, 2 * BLOCK), 1)
     base = me_r * blocks
-    for c in range(X_CHUNKS):
-        for a, src in enumerate((coef, direc)):
-            piece = src[:, c * part:(c + 1) * part].astype(jnp.float32).T.astype(jnp.bfloat16)
-            xall[pl.ds(base + c * per, per), :, a * orbs:(a + 1) * orbs] = piece.reshape(per, BLOCK, orbs)
-    lane = lax.broadcasted_iota(jnp.int32, (16, 2 * BLOCK), 1)
-
-    first = lax.broadcasted_iota(jnp.int32, (BLOCK // 2, 2 * BLOCK), 1) < BLOCK
-    to_smem[0].wait()
-    for k in range(pairs):
-        one, two = flat[smeta[0, 4, 2 * k]], flat[smeta[0, 4, 2 * k + 1]]
-        rows2[pl.ds(0, BLOCK // 2, stride=2), :] = jnp.where(first, one, pltpu.roll(two, BLOCK, 1))
-        rows2[pl.ds(1, BLOCK // 2, stride=2), :] = jnp.where(first, pltpu.roll(one, BLOCK, 1), two)
-        tall[0, k] = rows2[...].astype(jnp.bfloat16)
     pl.semaphore_wait(barrier, 2 + 1 + chips - 1)
 
     def x_ref(owner, c):
-        return xall.at[pl.ds(owner * blocks + c * per, per)]
+        return xall.at[c // X_CHUNKS, pl.ds(owner * blocks + c % X_CHUNKS * per, per)]
 
     def x_copy(owner, c, to, send, recv):
         return pltpu.make_async_remote_copy(
@@ -163,17 +157,28 @@
                     mats = tall[slot, 2 * g + u].reshape(BLOCK // 16, 16, 2 * BLOCK)
                     line.append((mats * keep[None]).reshape(BLOCK, 2 * BLOCK))
                 grid.append(jnp.concatenate(line, axis=1))
-            picked = jnp.concatenate([xall[smeta[slot, 1, 4 * g + i]] for i in range(4)], axis=0)
+            where = [smeta[slot, 1, 4 * g + i] for i in range(4)]
+            picked = jnp.concatenate([
+                jnp.concatenate([xall[a, c] for c in where], axis=0) for a in (0, 1)], axis=1)
             got = jnp.dot(jnp.concatenate(grid, axis=0), picked, preferred_element_type=jnp.float32)
             for a in range(4):
                 one = got[a * BLOCK:(a + 1) * BLOCK]
                 if carry is not None:
                     one = one + jnp.where(r[a] == before, carry, 0.0)
-                sums[4 * g + a] = one
+                sums[q * slots + 4 * g + a] = one
             carry, before = one, r[3]
-        for b in range(blocks):
-            at = slice(b * BLOCK, (b + 1) * BLOCK)
-            acc[at, :] += jnp.where(smeta[slot, 3, b] > 0, sums[smeta[slot, 2, b]], 0.0)
+
+    def add_rows(qs, begin):
+        def row(b, carry):
+            total = None if begin else acc[b]
+            for q in qs:
+                slot = slot_of(q)
+                one = jnp.where(smeta[slot, 3, b] > 0, sums[q * slots + smeta[slot, 2, b]], 0.0)
+                total = one if total is None else total + one
+            acc[b] = total
+            return carry
+
+        lax.fori_loop(0, blocks, row, 0, unroll=4)
 
     def send_ring(t):
         pieces, metas = ring_parts(t)
@@ -196,16 +201,17 @@
         for d in metas:
             to_smem[ring_slots(d, t)[1]].start()
 
-    for c in range(X_CHUNKS):
+    send_ring(1)
+    for i, (a, c) in enumerate(x_parts):
+        piece = (coef, direc)[a][:, c * part:(c + 1) * part].astype(jnp.float32).T.astype(jnp.bfloat16)
+        xall[a, pl.ds(base + c * per, per)] = piece.reshape(per, BLOCK, orbs)
         for k in range(1, chips):
-            cross_to(k, c).start()
-        if c == 0:
-            send_ring(1)
-    for c in range(X_CHUNKS):
-        sib_to(c).start()
-    acc[...] = jnp.zeros_like(acc)
-
-    events = [(((k - 1) * X_CHUNKS + c + 1) * 2.6, 0, k, c) for k in range(1, chips) for c in range(X_CHUNKS)]
+            cross_to(k, i).start()
+        sib_to(i).start()
+    to_smem[0].start()
+    to_smem[0].wait()
+
+    events = [(((k - 1) * len(x_parts) + c + 1) * 2.6, 0, k, c) for k in range(1, chips) for c in range(len(x_parts))]
     events += [(t * 3.9, 1, t, 0) for t in range(1, steps)]
     for _, kind, k, c in sorted(events):
         if kind == 0:
@@ -213,10 +219,10 @@
             fwd_to(k, c).start()
         else:
             ring_event(k)
-    for c in range(X_CHUNKS):
+    for c in range(len(x_parts)):
         sib_from(c).wait_recv()
     for k in range(1, chips):
-        for c in range(X_CHUNKS):
+        for c in range(len(x_parts)):
             fwd_from(k, c).wait_recv()
 
     for t in range(1, steps):
@@ -228,15 +234,17 @@
         return carry
 
     lax.fori_loop(0, n_col - 1, shard, 0)
+    add_rows(range(n_col - 1), True)
     ring_event(steps)
     to_smem[steps].wait()
     lax.fori_loop(n_col - 1, n_col, shard, 0)
+    add_rows((n_col - 1,), False)
 
     for a, out in enumerate((out_c, out_d)):
         for m in range(basis // 256):
-            out[:, m * 256:(m + 1) * 256] = acc[m * 256:(m + 1) * 256, a * orbs:(a + 1) * orbs].T.astype(jnp.bfloat16)
-
-    for c in range(X_CHUNKS):
+            out[:, m * 256:(m + 1) * 256] = acc[4 * m:4 * m + 4, :, a * orbs:(a + 1) * orbs].reshape(256, orbs).T.astype(jnp.bfloat16)
+
+    for c in range(len(x_parts)):
         sib_to(c).wait_send()
         for k in range(1, chips):
             cross_to(k, c).wait_send()
@@ -249,12 +257,9 @@
             ring(d, t, h).wait_send()
 
 
-def hand_over(a, b, out_a, out_b, sems):
-    copies = [pltpu.make_async_copy(src, dst, sems.at[i]) for i, (src, dst) in enumerate(((a, out_a), (b, out_b)))]
-    for copy in copies:
-        copy.start()
-    for copy in copies:
-        copy.wait()
+def hand_over(a, b, out_a, out_b):
+    out_a[...] = a[...]
+    out_b[...] = b[...]
 
 
 def local(n_row, n_col, coefs, direction, tiles, block_rows, block_cols, counts):
@@ -271,17 +276,17 @@
         in_specs=[vmem] * 5 + [pl.BlockSpec(memory_space=pltpu.SMEM)],
         out_specs=(vmem, vmem),
         scratch_shapes=[
-            pltpu.VMEM((n_row * basis // BLOCK, BLOCK, width), jnp.bfloat16),
+            pltpu.VMEM((2, n_row * basis // BLOCK, BLOCK, orbs), jnp.bfloat16),
             pltpu.VMEM((n_col, slots // 2, BLOCK, 2 * BLOCK), jnp.bfloat16),
             pltpu.VMEM((n_col, 8, 128), jnp.int32),
             pltpu.SMEM((n_col, 8, 128), jnp.int32),
-            pltpu.VMEM((slots, BLOCK, width), jnp.float32),
-            pltpu.VMEM((basis, width), jnp.float32),
+            pltpu.VMEM((n_col * slots, BLOCK, width), jnp.float32),
+            pltpu.VMEM((basis // BLOCK, BLOCK, width), jnp.float32),
             pltpu.VMEM((slots, BLOCK // 2, 2 * BLOCK), jnp.float32),
-            pltpu.VMEM((BLOCK, 2 * BLOCK), jnp.float32),
-            dma((X_CHUNKS,)), dma((X_CHUNKS,)),
-            dma((chips - 1, X_CHUNKS)), dma((chips - 1, X_CHUNKS)),
-            dma((chips - 1, X_CHUNKS)), dma((chips - 1, X_CHUNKS)),
+            pltpu.VMEM((slots // 2, BLOCK, 2 * BLOCK), jnp.float32),
+            dma((2 * X_CHUNKS,)), dma((2 * X_CHUNKS,)),
+            dma((chips - 1, 2 * X_CHUNKS)), dma((chips - 1, 2 * X_CHUNKS)),
+            dma((chips - 1, 2 * X_CHUNKS)), dma((chips - 1, 2 * X_CHUNKS)),
             dma((2, steps, HALVES)), dma((2, steps, HALVES)),
             dma((2, steps)), dma((2, steps)),
             dma((n_col,)),
@@ -293,9 +298,8 @@
     return tuple(pl.pallas_call(
         hand_over,
         out_shape=(out, out),
-        in_specs=[pl.BlockSpec(memory_space=pl.ANY)] * 2,
-        out_specs=(pl.BlockSpec(memory_space=pl.ANY),) * 2,
-        scratch_shapes=[dma((2,))],
+        in_specs=[vmem] * 2,
+        out_specs=(vmem, vmem),
         name="hand_over",
     )(*results))
 

time: 46.8 us -> 32.2 us (0.69)
  Pallas kernels: 45.4 us -> 30.8 us
    pallas_call x1, Pallas kernels: 17 us -> 1.84 us  [local(): pl.pallas_call(hand_over, out_shape=(out, out), in_specs=[vmem] * 2, out_...]
    pallas_call x1, Pallas kernels: 28.4 us -> 28.9 us  [local(): pl.pallas_call(functools.partial(kernel, n_row, n_col), out_shape=(out, o...]
where the time goes in v1:
time: 32.2 us; the launch traced here: 32 us
  Pallas kernels  30.8 us (96%)
  between operations  1.29 us (4%)
    pallas_call x1, Pallas kernels, local(): pl.pallas_call(functools.partial(kernel, n_row, n_col), out_shape=(out, o...  28.9 us
    pallas_call x1, Pallas kernels, local(): pl.pallas_call(hand_over, out_shape=(out, out), in_specs=[vmem] * 2, out_...  1.84 us

profile of v1, /device:TPU:0, one launch (start us, length us, event | category | flops | bytes accessed | tf_op | source)
XLA Modules:
  0.0 32.0 jit_solution(10335758796628944454)
XLA Ops:
  1.3 28.9 %block_sparse_apply.1 = (bf16[128,1024]{1,0:T(8,128)(2,1)}, bf16[128,1024]{1,0:T(8,128)(2,1)}) custom-call(bf16[128,1024]{1,0:T(8,128)(2,1)} %coef.1, bf16[128,1024]{1,0:T(8,128)(2,1)} %direc.1, bf16[1,24,4096]{2,1,0:T(8,128)(2,1)} %tiles.1, s32[1,24]{1,0:T(1,128)} %rows.1, s32[1,24]{1,0:T(1,128)} %cols.1, s32[1,1]{1,0:T(1,128)S(6)} %copy.8.counts), custom_call_target="tpu_custom_call" | custom-call | tf_op jit(solution)/shard_map/block_sparse_apply/pallas_call | solution.py:273
  30.2 1.8 %hand_over.1 = (bf16[128,1024]{1,0:T(8,128)(2,1)}, bf16[128,1024]{1,0:T(8,128)(2,1)}) custom-call(bf16[128,1024]{1,0:T(8,128)(2,1)} %get-tuple-element.4.a, bf16[128,1024]{1,0:T(8,128)(2,1)} %get-tuple-element.5.b), custom_call_target="tpu_custom_call" | custom-call | tf_op jit(solution)/shard_map/hand_over/pallas_call | solution.py:298

commit v2 on v1

--- a/solution.py
+++ b/solution.py
@@ -14,7 +14,7 @@
 
 
 def kernel(n_row, n_col, coef, direc, tiles, rows, cols, counts, out_c, out_d,
-           xall, tall, mall, smeta, sums, acc, flat, rows2,
+           x_coef, x_direc, tall, mall, smeta, sums, acc, flat, rows2,
            sib_s, sib_r, cross_s, cross_r, fwd_s, fwd_r, ring_s, ring_r, meta_s, meta_r, loc):
     orbs, basis = coef.shape
     width = 2 * orbs
@@ -26,6 +26,7 @@
     steps = n_col // 2
     part = basis // X_CHUNKS
     per = part // BLOCK
+    xall = (x_coef, x_direc)
     x_parts = [(a, c) for a in (0, 1) for c in range(X_CHUNKS)]
 
     me_r, me_c = lax.axis_index("row"), lax.axis_index("col")
@@ -84,7 +85,7 @@
     pl.semaphore_wait(barrier, 2 + 1 + chips - 1)
 
     def x_ref(owner, c):
-        return xall.at[c // X_CHUNKS, pl.ds(owner * blocks + c % X_CHUNKS * per, per)]
+        return xall[c // X_CHUNKS].at[pl.ds(owner * blocks + c % X_CHUNKS * per, per)]
 
     def x_copy(owner, c, to, send, recv):
         return pltpu.make_async_remote_copy(
@@ -138,7 +139,8 @@
     def slot_of(q):
         return (q % 2) * ((q + 1) // 2) + (1 - q % 2) * ((n_col - q // 2) % n_col)
 
-    def compute(q):
+    def compute(q, arrays):
+        lanes = slice(arrays[0] * orbs, (arrays[-1] + 1) * orbs)
         slot = slot_of(q)
         carry = None
         for g in range(slots // 4):
@@ -159,13 +161,13 @@
                 grid.append(jnp.concatenate(line, axis=1))
             where = [smeta[slot, 1, 4 * g + i] for i in range(4)]
             picked = jnp.concatenate([
-                jnp.concatenate([xall[a, c] for c in where], axis=0) for a in (0, 1)], axis=1)
+                jnp.concatenate([xall[a][c] for c in where], axis=0) for a in arrays], axis=1)
             got = jnp.dot(jnp.concatenate(grid, axis=0), picked, preferred_element_type=jnp.float32)
             for a in range(4):
                 one = got[a * BLOCK:(a + 1) * BLOCK]
                 if carry is not None:
                     one = one + jnp.where(r[a] == before, carry, 0.0)
-                sums[q * slots + 4 * g + a] = one
+                sums[q * slots + 4 * g + a, :, lanes] = one
             carry, before = one, r[3]
 
     def add_rows(qs, begin):
@@ -204,40 +206,56 @@
     send_ring(1)
     for i, (a, c) in enumerate(x_parts):
         piece = (coef, direc)[a][:, c * part:(c + 1) * part].astype(jnp.float32).T.astype(jnp.bfloat16)
-        xall[a, pl.ds(base + c * per, per)] = piece.reshape(per, BLOCK, orbs)
+        xall[a][pl.ds(base + c * per, per)] = piece.reshape(per, BLOCK, orbs)
         for k in range(1, chips):
             cross_to(k, i).start()
         sib_to(i).start()
     to_smem[0].start()
     to_smem[0].wait()
 
-    events = [(((k - 1) * len(x_parts) + c + 1) * 2.6, 0, k, c) for k in range(1, chips) for c in range(len(x_parts))]
-    events += [(t * 3.9, 1, t, 0) for t in range(1, steps)]
-    for _, kind, k, c in sorted(events):
-        if kind == 0:
-            cross_from(k, c).wait_recv()
-            fwd_to(k, c).start()
-        else:
-            ring_event(k)
-    for c in range(len(x_parts)):
-        sib_from(c).wait_recv()
-    for k in range(1, chips):
-        for c in range(len(x_parts)):
-            fwd_from(k, c).wait_recv()
-
-    for t in range(1, steps):
+    def shards(begin, end, arrays):
+        def shard(q, carry):
+            compute(q, arrays)
+            return carry
+
+        lax.fori_loop(begin, end, shard, 0)
+
+    def cross_events(a):
+        for i in range(a * X_CHUNKS, (a + 1) * X_CHUNKS):
+            for k in range(1, chips):
+                cross_from(k, i).wait_recv()
+                fwd_to(k, i).start()
+
+    def settle(a):
+        for i in range(a * X_CHUNKS, (a + 1) * X_CHUNKS):
+            sib_from(i).wait_recv()
+            for k in range(1, chips):
+                fwd_from(k, i).wait_recv()
+
+    def list_here(t):
         for d in (0, 1):
             to_smem[ring_slots(d, t)[1]].wait()
 
-    def shard(q, carry):
-        compute(q)
-        return carry
-
-    lax.fori_loop(0, n_col - 1, shard, 0)
+    ring_event(1)
+    cross_events(0)
+    settle(0)
+    list_here(1)
+    shards(0, 3, (0,))
+    ring_event(2)
+    list_here(2)
+    shards(3, 5, (0,))
+    cross_events(1)
+    for t in range(3, steps):
+        ring_event(t)
+    settle(1)
+    shards(0, 5, (1,))
+    for t in range(3, steps):
+        list_here(t)
+    shards(5, n_col - 1, (0, 1))
     add_rows(range(n_col - 1), True)
     ring_event(steps)
     to_smem[steps].wait()
-    lax.fori_loop(n_col - 1, n_col, shard, 0)
+    shards(n_col - 1, n_col, (0, 1))
     add_rows((n_col - 1,), False)
 
     for a, out in enumerate((out_c, out_d)):
@@ -276,7 +294,8 @@
         in_specs=[vmem] * 5 + [pl.BlockSpec(memory_space=pltpu.SMEM)],
         out_specs=(vmem, vmem),
         scratch_shapes=[
-            pltpu.VMEM((2, n_row * basis // BLOCK, BLOCK, orbs), jnp.bfloat16),
+            pltpu.VMEM((n_row * basis // BLOCK, BLOCK, orbs), jnp.bfloat16),
+            pltpu.VMEM((n_row * basis // BLOCK, BLOCK, orbs), jnp.bfloat16),
             pltpu.VMEM((n_col, slots // 2, BLOCK, 2 * BLOCK), jnp.bfloat16),
             pltpu.VMEM((n_col, 8, 128), jnp.int32),
             pltpu.SMEM((n_col, 8, 128), jnp.int32),

time: 32.2 us -> 32.3 us (level)
  no operation moved by 1% of the time
where the time goes in v2:
time: 32.3 us; the launch traced here: 32.1 us
  Pallas kernels  30.9 us (96%)
  between operations  1.29 us (4%)
    pallas_call x1, Pallas kernels, local(): pl.pallas_call(functools.partial(kernel, n_row, n_col), out_shape=(out, o...  29 us
    pallas_call x1, Pallas kernels, local(): pl.pallas_call(hand_over, out_shape=(out, out), in_specs=[vmem] * 2, out_...  1.84 us

profile of v2, /device:TPU:0, one launch (start us, length us, event | category | flops | bytes accessed | tf_op | source)
XLA Modules:
  0.0 32.1 jit_solution(11117403178572158759)
XLA Ops:
  1.3 29.0 %block_sparse_apply.1 = (bf16[128,1024]{1,0:T(8,128)(2,1)}, bf16[128,1024]{1,0:T(8,128)(2,1)}) custom-call(bf16[128,1024]{1,0:T(8,128)(2,1)} %coef.1, bf16[128,1024]{1,0:T(8,128)(2,1)} %direc.1, bf16[1,24,4096]{2,1,0:T(8,128)(2,1)} %tiles.1, s32[1,24]{1,0:T(1,128)} %rows.1, s32[1,24]{1,0:T(1,128)} %cols.1, s32[1,1]{1,0:T(1,128)S(6)} %copy.8.counts), custom_call_target="tpu_custom_call" | custom-call | tf_op jit(solution)/shard_map/block_sparse_apply/pallas_call | solution.py:291
  30.3 1.8 %hand_over.1 = (bf16[128,1024]{1,0:T(8,128)(2,1)}, bf16[128,1024]{1,0:T(8,128)(2,1)}) custom-call(bf16[128,1024]{1,0:T(8,128)(2,1)} %get-tuple-element.4.a, bf16[128,1024]{1,0:T(8,128)(2,1)} %get-tuple-element.5.b), custom_call_target="tpu_custom_call" | custom-call | tf_op jit(solution)/shard_map/hand_over/pallas_call | solution.py:317

commit v3 on v2

--- a/solution.py
+++ b/solution.py
@@ -220,11 +220,10 @@
 
         lax.fori_loop(begin, end, shard, 0)
 
-    def cross_events(a):
-        for i in range(a * X_CHUNKS, (a + 1) * X_CHUNKS):
-            for k in range(1, chips):
-                cross_from(k, i).wait_recv()
-                fwd_to(k, i).start()
+    def cross_event(i):
+        for k in range(1, chips):
+            cross_from(k, i).wait_recv()
+            fwd_to(k, i).start()
 
     def settle(a):
         for i in range(a * X_CHUNKS, (a + 1) * X_CHUNKS):
@@ -237,16 +236,18 @@
             to_smem[ring_slots(d, t)[1]].wait()
 
     ring_event(1)
-    cross_events(0)
+    for i in range(X_CHUNKS):
+        cross_event(i)
+    ring_event(2)
     settle(0)
     list_here(1)
-    shards(0, 3, (0,))
-    ring_event(2)
     list_here(2)
-    shards(3, 5, (0,))
-    cross_events(1)
+    for i in range(X_CHUNKS, 2 * X_CHUNKS - 1):
+        cross_event(i)
+    shards(0, 5, (0,))
     for t in range(3, steps):
         ring_event(t)
+    cross_event(2 * X_CHUNKS - 1)
     settle(1)
     shards(0, 5, (1,))
     for t in range(3, steps):
@@ -275,9 +276,21 @@
             ring(d, t, h).wait_send()
 
 
-def hand_over(a, b, out_a, out_b):
-    out_a[...] = a[...]
-    out_b[...] = b[...]
+def hand_over(a, b, out_a, out_b, held, came, gone):
+    half = a.shape[0] // 2
+    here, there = [], []
+    for i, (src, dst) in enumerate(((a, out_a), (b, out_b))):
+        for h in (0, 1):
+            at = pl.ds(h * half, half)
+            n = 2 * i + h
+            here.append(pltpu.make_async_copy(src.at[at], held.at[n], came.at[n]))
+            there.append(pltpu.make_async_copy(held.at[n], dst.at[at], gone.at[n]))
+            here[-1].start()
+    for one, two in zip(here, there):
+        one.wait()
+        two.start()
+    for two in there:
+        two.wait()
 
 
 def local(n_row, n_col, coefs, direction, tiles, block_rows, block_cols, counts):
@@ -317,8 +330,9 @@
     return tuple(pl.pallas_call(
         hand_over,
         out_shape=(out, out),
-        in_specs=[vmem] * 2,
-        out_specs=(vmem, vmem),
+        in_specs=[pl.BlockSpec(memory_space=pl.ANY)] * 2,
+        out_specs=(pl.BlockSpec(memory_space=pl.ANY),) * 2,
+        scratch_shapes=[pltpu.VMEM((4, orbs // 2, basis), jnp.bfloat16), dma((4,)), dma((4,))],
         name="hand_over",
     )(*results))
 

time: 32.3 us -> 31.6 us (0.978)
  the two profiles are of different devices: /device:TPU:0 before, /device:TPU:1 now
where the time goes in v3:
time: 31.6 us; the launch traced here: 31.4 us
  Pallas kernels  30.1 us (95%)
  between operations  1.29 us (4%)
    pallas_call x1, Pallas kernels, local(): pl.pallas_call(functools.partial(kernel, n_row, n_col), out_shape=(out, o...  28.3 us
    pallas_call x1, Pallas kernels, local(): pl.pallas_call(hand_over, out_shape=(out, out), in_specs=[pl.BlockSpec(me...  1.82 us

profile of v3, /device:TPU:1, one launch (start us, length us, event | category | flops | bytes accessed | tf_op | source)
XLA Modules:
  0.0 31.4 jit_solution(5734881355034438254)
XLA Ops:
  1.3 28.3 %block_sparse_apply.1 = (bf16[128,1024]{1,0:T(8,128)(2,1)}, bf16[128,1024]{1,0:T(8,128)(2,1)}) custom-call(bf16[128,1024]{1,0:T(8,128)(2,1)} %coef.1, bf16[128,1024]{1,0:T(8,128)(2,1)} %direc.1, bf16[1,24,4096]{2,1,0:T(8,128)(2,1)} %tiles.1, s32[1,24]{1,0:T(1,128)} %rows.1, s32[1,24]{1,0:T(1,128)} %cols.1, s32[1,1]{1,0:T(1,128)S(6)} %copy.8.counts), custom_call_target="tpu_custom_call" | custom-call | tf_op jit(solution)/shard_map/block_sparse_apply/pallas_call | solution.py:304
  29.6 1.8 %hand_over.1 = (bf16[128,1024]{1,0:T(8,128)(2,1)}, bf16[128,1024]{1,0:T(8,128)(2,1)}) custom-call(bf16[128,1024]{1,0:T(8,128)(2,1)} %get-tuple-element.4.a, bf16[128,1024]{1,0:T(8,128)(2,1)} %get-tuple-element.5.b), custom_call_target="tpu_custom_call" | custom-call | tf_op jit(solution)/shard_map/hand_over/pallas_call | solution.py:330

commit v4 on v3

--- a/solution.py
+++ b/solution.py
@@ -48,40 +48,11 @@
     for k in range(1, chips):
         pl.semaphore_signal(barrier, inc=1, device_id=(((chip + k) % chips) * 2 + core, me_c), device_id_type=MESH)
 
-    lane1 = lax.broadcasted_iota(jnp.int32, (1, 128), 1)
-    pad = lax.broadcasted_iota(jnp.int32, (8, 128), 0)
-    row_key = jnp.where(lane1[:, :slots] < counts[0, 0], rows[...], blocks)
-    mall[0] = jnp.zeros((8, 128), jnp.int32)
-    mall[0, 0:1, 0:slots] = row_key * slots + lane1[:, :slots]
-    mall[0, 1:2, 0:slots] = cols[...]
-    mall[0, 2:3, 0:slots] = row_key
-    wide = mall[0]
-    tall_form = wide.T
-    key_col, col_col, row_col = (tall_form[:slots, i:i + 1] for i in range(3))
-    rank = jnp.sum((key_col < wide[0:1]).astype(jnp.int32), axis=0, keepdims=True)
-    moves = jnp.where(rank[:, :slots] == lax.broadcasted_iota(jnp.int32, (slots, slots), 0), 1.0, 0.0)
-    in_order = jnp.dot(moves.astype(jnp.bfloat16), tiles[0], preferred_element_type=jnp.float32)
-    for m in range(BLOCK // 2):
-        flat[:, m, :] = in_order[:, m * 2 * BLOCK:(m + 1) * 2 * BLOCK]
-    first = lax.broadcasted_iota(jnp.int32, (BLOCK // 2, 2 * BLOCK), 1) < BLOCK
-    for k in range(pairs):
-        one, two = flat[2 * k], flat[2 * k + 1]
-        rows2[k, pl.ds(0, BLOCK // 2, stride=2), :] = jnp.where(first, one, pltpu.roll(two, BLOCK, 1))
-        rows2[k, pl.ds(1, BLOCK // 2, stride=2), :] = jnp.where(first, pltpu.roll(one, BLOCK, 1), two)
-        tall[0, k] = rows2[k].astype(jnp.bfloat16)
-    rank_col = jnp.where(pad == 0, rank, 0).T[:slots, 0:1]
-    hit = rank_col == lane1
-
-    def pull(values):
-        return jnp.sum(jnp.where(hit, values, 0), axis=0, keepdims=True)
-
-    upto = jnp.sum((row_col <= lane1).astype(jnp.int32), axis=0, keepdims=True)
-    have = jnp.sum((row_col == lane1).astype(jnp.int32), axis=0, keepdims=True)
-    for i, values in enumerate((pull(row_col), pull(col_col), jnp.maximum(upto - 1, 0), have)):
-        mall[0, i:i + 1] = values
-    to_smem = [pltpu.make_async_copy(mall.at[i], smeta.at[i], loc.at[i]) for i in range(n_col)]
     lane = lax.broadcasted_iota(jnp.int32, (16, 2 * BLOCK), 1)
     base = me_r * blocks
+    for a, c in x_parts:
+        piece = (coef, direc)[a][:, c * part:(c + 1) * part].T
+        xall[a][pl.ds(base + c * per, per)] = piece.reshape(per, BLOCK, orbs)
     pl.semaphore_wait(barrier, 2 + 1 + chips - 1)
 
     def x_ref(owner, c):
@@ -203,13 +174,45 @@
         for d in metas:
             to_smem[ring_slots(d, t)[1]].start()
 
-    send_ring(1)
-    for i, (a, c) in enumerate(x_parts):
-        piece = (coef, direc)[a][:, c * part:(c + 1) * part].astype(jnp.float32).T.astype(jnp.bfloat16)
-        xall[a][pl.ds(base + c * per, per)] = piece.reshape(per, BLOCK, orbs)
+    for i in range(len(x_parts)):
         for k in range(1, chips):
             cross_to(k, i).start()
         sib_to(i).start()
+
+    lane1 = lax.broadcasted_iota(jnp.int32, (1, 128), 1)
+    pad = lax.broadcasted_iota(jnp.int32, (8, 128), 0)
+    row_key = jnp.where(lane1[:, :slots] < counts[0, 0], rows[...], blocks)
+    mall[0] = jnp.zeros((8, 128), jnp.int32)
+    mall[0, 0:1, 0:slots] = row_key * slots + lane1[:, :slots]
+    mall[0, 1:2, 0:slots] = cols[...]
+    mall[0, 2:3, 0:slots] = row_key
+    wide = mall[0]
+    tall_form = wide.T
+    key_col, col_col, row_col = (tall_form[:slots, i:i + 1] for i in range(3))
+    rank = jnp.sum((key_col < wide[0:1]).astype(jnp.int32), axis=0, keepdims=True)
+    moves = jnp.where(rank[:, :slots] == lax.broadcasted_iota(jnp.int32, (slots, slots), 0), 1.0, 0.0)
+    in_order = jnp.dot(moves.astype(jnp.bfloat16), tiles[0], preferred_element_type=jnp.float32)
+    for m in range(BLOCK // 2):
+        flat[:, m, :] = in_order[:, m * 2 * BLOCK:(m + 1) * 2 * BLOCK]
+    first = lax.broadcasted_iota(jnp.int32, (BLOCK // 2, 2 * BLOCK), 1) < BLOCK
+    for k in range(pairs):
+        one, two = flat[2 * k], flat[2 * k + 1]
+        rows2[k, pl.ds(0, BLOCK // 2, stride=2), :] = jnp.where(first, one, pltpu.roll(two, BLOCK, 1))
+        rows2[k, pl.ds(1, BLOCK // 2, stride=2), :] = jnp.where(first, pltpu.roll(one, BLOCK, 1), two)
+        tall[0, k] = rows2[k].astype(jnp.bfloat16)
+    rank_col = jnp.where(pad == 0, rank, 0).T[:slots, 0:1]
+    hit = rank_col == lane1
+
+    def pull(values):
+        return jnp.sum(jnp.where(hit, values, 0), axis=0, keepdims=True)
+
+    upto = jnp.sum((row_col <= lane1).astype(jnp.int32), axis=0, keepdims=True)
+    have = jnp.sum((row_col == lane1).astype(jnp.int32), axis=0, keepdims=True)
+    for i, values in enumerate((pull(row_col), pull(col_col), jnp.maximum(upto - 1, 0), have)):
+        mall[0, i:i + 1] = values
+    to_smem = [pltpu.make_async_copy(mall.at[i], smeta.at[i], loc.at[i]) for i in range(n_col)]
+
+    send_ring(1)
     to_smem[0].start()
     to_smem[0].wait()
 
@@ -235,21 +238,24 @@
         for d in (0, 1):
             to_smem[ring_slots(d, t)[1]].wait()
 
+    cross_event(0)
     ring_event(1)
-    for i in range(X_CHUNKS):
+    for i in range(1, X_CHUNKS):
+        cross_event(i)
+    settle(0)
+    list_here(1)
+    shards(0, 3, (0,))
+    for i in range(X_CHUNKS, 2 * X_CHUNKS - 1):
         cross_event(i)
     ring_event(2)
-    settle(0)
-    list_here(1)
     list_here(2)
-    for i in range(X_CHUNKS, 2 * X_CHUNKS - 1):
-        cross_event(i)
-    shards(0, 5, (0,))
+    shards(3, 5, (0,))
+    cross_event(2 * X_CHUNKS - 1)
+    settle(1)
+    shards(0, 2, (1,))
     for t in range(3, steps):
         ring_event(t)
-    cross_event(2 * X_CHUNKS - 1)
-    settle(1)
-    shards(0, 5, (1,))
+    shards(2, 5, (1,))
     for t in range(3, steps):
         list_here(t)
     shards(5, n_col - 1, (0, 1))
@@ -261,7 +267,7 @@
 
     for a, out in enumerate((out_c, out_d)):
         for m in range(basis // 256):
-            out[:, m * 256:(m + 1) * 256] = acc[4 * m:4 * m + 4, :, a * orbs:(a + 1) * orbs].reshape(256, orbs).T.astype(jnp.bfloat16)
+            out[:, m * 256:(m + 1) * 256] = acc[4 * m:4 * m + 4, :, a * orbs:(a + 1) * orbs].reshape(256, orbs).astype(jnp.bfloat16).T
 
     for c in range(len(x_parts)):
         sib_to(c).wait_send()

time: 31.6 us -> 32.4 us (1.025)
  the two profiles are of different devices: /device:TPU:1 before, /device:TPU:0 now
where the time goes in v4:
time: 32.4 us; the launch traced here: 32.2 us
  Pallas kernels  30.9 us (95%)
  between operations  1.29 us (4%)
    pallas_call x1, Pallas kernels, local(): pl.pallas_call(functools.partial(kernel, n_row, n_col), out_shape=(out, o...  29.1 us
    pallas_call x1, Pallas kernels, local(): pl.pallas_call(hand_over, out_shape=(out, out), in_specs=[pl.BlockSpec(me...  1.82 us

profile of v4, /device:TPU:0, one launch (start us, length us, event | category | flops | bytes accessed | tf_op | source)
XLA Modules:
  0.0 32.2 jit_solution(6890048728543759684)
XLA Ops:
  1.3 29.1 %block_sparse_apply.1 = (bf16[128,1024]{1,0:T(8,128)(2,1)}, bf16[128,1024]{1,0:T(8,128)(2,1)}) custom-call(bf16[128,1024]{1,0:T(8,128)(2,1)} %coef.1, bf16[128,1024]{1,0:T(8,128)(2,1)} %direc.1, bf16[1,24,4096]{2,1,0:T(8,128)(2,1)} %tiles.1, s32[1,24]{1,0:T(1,128)} %rows.1, s32[1,24]{1,0:T(1,128)} %cols.1, s32[1,1]{1,0:T(1,128)S(6)} %copy.8.counts), custom_call_target="tpu_custom_call" | custom-call | tf_op jit(solution)/shard_map/block_sparse_apply/pallas_call | solution.py:310
  30.4 1.8 %hand_over.1 = (bf16[128,1024]{1,0:T(8,128)(2,1)}, bf16[128,1024]{1,0:T(8,128)(2,1)}) custom-call(bf16[128,1024]{1,0:T(8,128)(2,1)} %get-tuple-element.4.a, bf16[128,1024]{1,0:T(8,128)(2,1)} %get-tuple-element.5.b), custom_call_target="tpu_custom_call" | custom-call | tf_op jit(solution)/shard_map/hand_over/pallas_call | solution.py:336

commit v5 on v3

--- a/solution.py
+++ b/solution.py
@@ -9,7 +9,7 @@
 
 BLOCK = 64
 X_CHUNKS = 2
-HALVES = 2
+RING_CUTS = 4
 MESH = pl.DeviceIdType.MESH
 
 
@@ -21,7 +21,7 @@
     slots = rows.shape[1]
     blocks = basis // BLOCK
     pairs = slots // 2
-    cut_pairs = pairs // HALVES
+    cut_pairs = pairs // RING_CUTS
     chips = n_row // 2
     steps = n_col // 2
     part = basis // X_CHUNKS
@@ -133,8 +133,8 @@
 
     def ring_parts(t):
         if t < steps:
-            return [(d, h) for h in range(HALVES) for d in (0, 1)], (0, 1)
-        return [(0, 0), (1, 1)], (0,)
+            return [(d, h) for h in range(RING_CUTS) for d in (0, 1)], (0, 1)
+        return [(h % 2, h) for h in range(RING_CUTS)], (0,)
 
     def slot_of(q):
         return (q % 2) * ((q + 1) // 2) + (1 - q % 2) * ((n_col - q // 2) % n_col)
@@ -205,7 +205,7 @@
 
     send_ring(1)
     for i, (a, c) in enumerate(x_parts):
-        piece = (coef, direc)[a][:, c * part:(c + 1) * part].astype(jnp.float32).T.astype(jnp.bfloat16)
+        piece = (coef, direc)[a][:, c * part:(c + 1) * part].T
         xall[a][pl.ds(base + c * per, per)] = piece.reshape(per, BLOCK, orbs)
         for k in range(1, chips):
             cross_to(k, i).start()
@@ -244,15 +244,15 @@
     list_here(2)
     for i in range(X_CHUNKS, 2 * X_CHUNKS - 1):
         cross_event(i)
-    shards(0, 5, (0,))
+    shards(0, 3, (0,))
     for t in range(3, steps):
         ring_event(t)
     cross_event(2 * X_CHUNKS - 1)
     settle(1)
-    shards(0, 5, (1,))
+    shards(0, 3, (1,))
     for t in range(3, steps):
         list_here(t)
-    shards(5, n_col - 1, (0, 1))
+    shards(3, n_col - 1, (0, 1))
     add_rows(range(n_col - 1), True)
     ring_event(steps)
     to_smem[steps].wait()
@@ -261,7 +261,7 @@
 
     for a, out in enumerate((out_c, out_d)):
         for m in range(basis // 256):
-            out[:, m * 256:(m + 1) * 256] = acc[4 * m:4 * m + 4, :, a * orbs:(a + 1) * orbs].reshape(256, orbs).T.astype(jnp.bfloat16)
+            out[:, m * 256:(m + 1) * 256] = acc[4 * m:4 * m + 4, :, a * orbs:(a + 1) * orbs].reshape(256, orbs).astype(jnp.bfloat16).T
 
     for c in range(len(x_parts)):
         sib_to(c).wait_send()
@@ -319,7 +319,7 @@
             dma((2 * X_CHUNKS,)), dma((2 * X_CHUNKS,)),
             dma((chips - 1, 2 * X_CHUNKS)), dma((chips - 1, 2 * X_CHUNKS)),
             dma((chips - 1, 2 * X_CHUNKS)), dma((chips - 1, 2 * X_CHUNKS)),
-            dma((2, steps, HALVES)), dma((2, steps, HALVES)),
+            dma((2, steps, RING_CUTS)), dma((2, steps, RING_CUTS)),
             dma((2, steps)), dma((2, steps)),
             dma((n_col,)),
         ],

time: 31.6 us -> 30.8 us (0.975)
  Pallas kernels: 30.1 us -> 29.3 us
    pallas_call x1, Pallas kernels: 28.3 us -> 27.5 us  [local(): pl.pallas_call(functools.partial(kernel, n_row, n_col), out_shape=(out, o...]
where the time goes in v5:
time: 30.8 us; the launch traced here: 30.6 us
  Pallas kernels  29.3 us (95%)
  between operations  1.29 us (4%)
    pallas_call x1, Pallas kernels, local(): pl.pallas_call(functools.partial(kernel, n_row, n_col), out_shape=(out, o...  27.5 us
    pallas_call x1, Pallas kernels, local(): pl.pallas_call(hand_over, out_shape=(out, out), in_specs=[pl.BlockSpec(me...  1.82 us

profile of v5, /device:TPU:1, one launch (start us, length us, event | category | flops | bytes accessed | tf_op | source)
XLA Modules:
  0.0 30.6 jit_solution(2805401120099077330)
XLA Ops:
  1.3 27.5 %block_sparse_apply.1 = (bf16[128,1024]{1,0:T(8,128)(2,1)}, bf16[128,1024]{1,0:T(8,128)(2,1)}) custom-call(bf16[128,1024]{1,0:T(8,128)(2,1)} %coef.1, bf16[128,1024]{1,0:T(8,128)(2,1)} %direc.1, bf16[1,24,4096]{2,1,0:T(8,128)(2,1)} %tiles.1, s32[1,24]{1,0:T(1,128)} %rows.1, s32[1,24]{1,0:T(1,128)} %cols.1, s32[1,1]{1,0:T(1,128)S(6)} %copy.8.counts), custom_call_target="tpu_custom_call" | custom-call | tf_op jit(solution)/shard_map/block_sparse_apply/pallas_call | solution.py:304
  28.8 1.8 %hand_over.1 = (bf16[128,1024]{1,0:T(8,128)(2,1)}, bf16[128,1024]{1,0:T(8,128)(2,1)}) custom-call(bf16[128,1024]{1,0:T(8,128)(2,1)} %get-tuple-element.4.a, bf16[128,1024]{1,0:T(8,128)(2,1)} %get-tuple-element.5.b), custom_call_target="tpu_custom_call" | custom-call | tf_op jit(solution)/shard_map/hand_over/pallas_call | solution.py:330
